TPU v7x, 32 devices: a whole 2x2x4 slice. The times are simulated.
32 devices in a mesh: batch: 16 (over z, y, x), mp: 2 (over core).
Axes of the slice: x: 2, y: 2, z: 4, core: 2. Of those that a mesh axis runs over, the one named last changes fastest.
Arguments:
- image_patches: bfloat16 [128, 50, 768], P('batch'), may hold values from -6 to 6
- text_rows: bfloat16 [128, 16, 768], P('batch'), may hold values from -6 to 6
- text_mask: int32 [128, 16], P('batch'), may hold values from 0 to 1, as said below
- image_qkv: bfloat16 [768, 3, 768], P(None, None, 'mp'), may hold values from -0.21875 to 0.21875
- image_out: bfloat16 [768, 768], P('mp'), may hold values from -0.875 to 0.875
- image_up: bfloat16 [768, 3072], P(None, 'mp'), may hold values from -0.21875 to 0.21875
- image_down: bfloat16 [3072, 768], P('mp'), may hold values from -0.109375 to 0.109375
- text_gain_one: float32 [768], replicated, may hold values from 0.5 to 1.5
- text_gain_two: float32 [768], replicated, may hold values from 0.5 to 1.5
- text_qkv: bfloat16 [768, 3, 768], P(None, None, 'mp'), may hold values from -0.21875 to 0.21875
- text_out: bfloat16 [768, 768], P('mp'), may hold values from -0.625 to 0.625
- text_up: bfloat16 [768, 3072], P(None, 'mp'), may hold values from -0.21875 to 0.21875
- text_down: bfloat16 [3072, 768], P('mp'), may hold values from -0.109375 to 0.109375
- text_proj: bfloat16 [768, 768], P(None, 'mp'), may hold values from -0.21875 to 0.21875
- log_temp: float32 [], replicated, may hold values from 3.5 to 4.2
Outputs:
- loss: float32 [], replicated
- grad_text_rows: float32 [128, 16, 768], P('batch')
- grad_gain_one: float32 [768], P('mp')
- grad_gain_two: float32 [768], P('mp')
- grad_qkv: float32 [768, 3, 768], P(None, None, 'mp')
- grad_out: float32 [768, 768], P('mp')
- grad_up: float32 [768, 3072], P(None, 'mp')
- grad_down: float32 [3072, 768], P('mp')
- grad_proj: float32 [768, 768], P(None, 'mp')
- grad_log_temp: float32 [], replicated
Inputs may be any that keep to these rules, and one draw needn't show every extreme that they name: `text_mask`: each row holds ones on a prefix of 4 to 16 positions and zeros after it.
All inputs are finite; a program needn't handle non-finite values.
Results may differ from a plain program's by a relative error of at most 0.01.
Values sent between devices are 32-bit elements; how exact they have to be, the bound alone decides.
A program may use at most 128 MiB of HBM per device.

v0:
```python
import jax
import jax.numpy as jnp
from jax import lax
from jax.sharding import PartitionSpec as P

HEAD = 64


LN_EPS = 1e-06
NORM_EPS = 1e-06
HIGHEST = lax.Precision.HIGHEST


def layer_norm(rows):
    center = rows - jnp.mean(rows, -1, keepdims=True)
    spread = jnp.mean(center * center, -1, keepdims=True)
    return center * lax.rsqrt(spread + LN_EPS)


def unit_rows(rows):
    return rows * lax.rsqrt(jnp.sum(rows * rows, -1, keepdims=True) + NORM_EPS)


def exact_gelu(values):
    return jax.nn.gelu(values, approximate=False)


def online_merge(row_top, logits):
    new_top = jnp.maximum(row_top, jnp.max(logits, -1))
    new_total = jnp.sum(jnp.exp(logits - new_top[:, None]), -1)
    return (new_top, new_total)


def block_forward(hidden, key_mask, gain_first, gain_second, w_qkv, w_out, w_up, w_down, is_image):
    pair_count, length, model_width = hidden.shape
    flat_rows = hidden.reshape(pair_count * length, model_width)
    normed = (layer_norm(flat_rows) * gain_first).astype(jnp.bfloat16)
    local_heads = w_qkv.shape[2] // HEAD
    packed = jnp.einsum("rd,dcf->rcf", normed, w_qkv, preferred_element_type=jnp.float32).astype(
        jnp.bfloat16
    )
    split_heads = packed.reshape(pair_count, length, 3, local_heads, HEAD)
    queries = split_heads[:, :, 0]
    key_rows = split_heads[:, :, 1]
    value_rows = split_heads[:, :, 2]
    scores = jnp.einsum(
        "nqhe,nkhe->nhqk", queries, key_rows, preferred_element_type=jnp.float32
    ) * HEAD ** (-0.5)
    scores = jnp.where(key_mask[:, None, None, :], scores, -1000000000.0)
    row_top = jnp.max(scores, -1, keepdims=True)
    raised = jnp.exp(scores - row_top)
    row_total = jnp.sum(raised, -1, keepdims=True)
    softmax_rows = raised / row_total
    log_total = row_top + jnp.log(row_total)
    mixed_rows = jnp.einsum(
        "nhqk,nkhe->nqhe",
        softmax_rows.astype(jnp.bfloat16),
        value_rows,
        preferred_element_type=jnp.float32,
    )
    mixed_rows = mixed_rows.astype(jnp.bfloat16).reshape(pair_count * length, local_heads * HEAD)
    partial_out = jnp.dot(mixed_rows, w_out, preferred_element_type=jnp.float32)
    if is_image:
        attended = lax.psum(partial_out, "mp")
    else:
        attended = lax.psum(partial_out, "mp")
    first_sum = flat_rows + attended
    normed_two = (layer_norm(first_sum) * gain_second).astype(jnp.bfloat16)
    upward = jnp.dot(normed_two, w_up, preferred_element_type=jnp.float32)
    activated = exact_gelu(upward).astype(jnp.bfloat16)
    partial_down = jnp.dot(activated, w_down, preferred_element_type=jnp.float32)
    if is_image:
        downward = lax.psum(partial_down, "mp")
    else:
        downward = lax.psum(partial_down, "mp")
    second = first_sum + downward
    kept_values = (
        normed,
        queries,
        key_rows,
        value_rows,
        log_total,
        mixed_rows,
        first_sum,
        normed_two,
        upward,
        activated,
    )
    return (second, kept_values)


def per_device(
    image_patches,
    text_rows,
    text_mask,
    image_qkv,
    image_out,
    image_up,
    image_down,
    text_gain_one,
    text_gain_two,
    text_qkv,
    text_out,
    text_up,
    text_down,
    text_proj,
    log_temp,
):
    pair_count = text_rows.shape[0]
    length = text_rows.shape[1]
    model_width = text_rows.shape[2]
    ones_gain = jnp.ones((model_width,), jnp.float32)
    every_patch = jnp.ones(image_patches.shape[:2], dtype=bool)
    image_rows, unused = block_forward(
        image_patches.astype(jnp.float32),
        every_patch,
        ones_gain,
        ones_gain,
        image_qkv,
        image_out,
        image_up,
        image_down,
        True,
    )
    image_norm = unit_rows(jnp.mean(image_rows.reshape(pair_count, -1, model_width), 1))
    valid_keys = text_mask > 0
    text_hidden = text_rows.astype(jnp.float32)
    second, kept_values = block_forward(
        text_hidden,
        valid_keys,
        text_gain_one,
        text_gain_two,
        text_qkv,
        text_out,
        text_up,
        text_down,
        False,
    )
    (
        normed,
        queries,
        key_rows,
        value_rows,
        log_total,
        mixed_rows,
        first_sum,
        normed_two,
        upward,
        activated,
    ) = kept_values
    mask_float = text_mask.astype(jnp.float32)
    token_count = jnp.sum(mask_float, 1, keepdims=True)
    second_rows = second.reshape(pair_count, length, model_width)
    pooled = jnp.sum(second_rows * mask_float[:, :, None], 1) / token_count
    pooled_low = pooled.astype(jnp.bfloat16)
    embed_half = jnp.dot(pooled_low, text_proj, preferred_element_type=jnp.float32)
    embed_full = lax.all_gather(embed_half, "mp", axis=1, tiled=True)
    text_norm = unit_rows(embed_full)
    scale = jnp.exp(log_temp)
    total_pairs = pair_count * lax.axis_size("batch")
    my_rows = lax.axis_index("batch") * pair_count + jnp.arange(pair_count, dtype=jnp.int32)
    start_top = jnp.full((pair_count,), -1e30, jnp.float32)
    zero_rows = jnp.zeros((pair_count,), jnp.float32)
    forward_init = (start_top, zero_rows, start_top, zero_rows)
    image_piece = lax.all_gather(image_norm, "batch", axis=0, tiled=True)
    text_piece = lax.all_gather(text_norm, "batch", axis=0, tiled=True)
    text_logits = scale * jnp.dot(
        text_norm, image_piece.T, precision=HIGHEST, preferred_element_type=jnp.float32
    )
    image_logits = scale * jnp.dot(
        image_norm, text_piece.T, precision=HIGHEST, preferred_element_type=jnp.float32
    )
    text_top, text_total = online_merge(forward_init[0], text_logits)
    image_top, image_total = online_merge(forward_init[2], image_logits)
    text_lse = text_top + jnp.log(text_total)
    image_lse = image_top + jnp.log(image_total)
    image_piece = lax.all_gather(image_norm, "batch", axis=0, tiled=True)
    lse_piece = lax.all_gather(image_lse, "batch", axis=0, tiled=True)
    cosine = jnp.dot(
        text_norm, image_piece.T, precision=HIGHEST, preferred_element_type=jnp.float32
    )
    logits = scale * cosine
    columns = jnp.arange(image_piece.shape[0], dtype=jnp.int32)
    diagonal = (columns[None, :] == my_rows[:, None]).astype(jnp.float32)
    pair_grad = (
        jnp.exp(logits - text_lse[:, None]) + jnp.exp(logits - lse_piece[None, :]) - 2.0 * diagonal
    ) / (2.0 * total_pairs)
    grad_norm = scale * jnp.dot(
        pair_grad, image_piece, precision=HIGHEST, preferred_element_type=jnp.float32
    )
    temp_part = jnp.sum(pair_grad * cosine)
    grad_norm, temp_part = (grad_norm, temp_part)
    loss_part = (
        jnp.sum(text_lse) + jnp.sum(image_lse) - 2.0 * scale * jnp.sum(text_norm * image_norm)
    )
    loss_sum, temp_sum = lax.psum((loss_part, temp_part), "batch")
    loss = loss_sum / (2.0 * total_pairs)
    grad_log_temp = scale * temp_sum
    unused_norm, norm_pull = jax.vjp(unit_rows, embed_full)
    grad_embed = norm_pull(grad_norm)[0]
    mp_index = lax.axis_index("mp")
    half_width = text_proj.shape[1]
    grad_half = lax.dynamic_slice_in_dim(grad_embed, mp_index * half_width, half_width, 1).astype(
        jnp.bfloat16
    )
    grad_proj = jnp.einsum("pd,pf->df", pooled_low, grad_half, preferred_element_type=jnp.float32)
    grad_pooled = lax.psum(
        jnp.einsum("pf,df->pd", grad_half, text_proj, preferred_element_type=jnp.float32), "mp"
    )
    pool_weights = mask_float / token_count
    grad_second = (pool_weights[:, :, None] * grad_pooled[:, None, :]).reshape(
        pair_count * length, model_width
    )
    grad_down_in = grad_second.astype(jnp.bfloat16)
    grad_down = jnp.einsum("rf,rd->fd", activated, grad_down_in, preferred_element_type=jnp.float32)
    grad_act = jnp.einsum("rd,fd->rf", grad_down_in, text_down, preferred_element_type=jnp.float32)
    unused_gelu, gelu_pull = jax.vjp(exact_gelu, upward)
    grad_up_in = gelu_pull(grad_act)[0].astype(jnp.bfloat16)
    grad_up = jnp.einsum("rd,rf->df", normed_two, grad_up_in, preferred_element_type=jnp.float32)
    grad_normed_two = lax.psum(
        jnp.einsum("rf,df->rd", grad_up_in, text_up, preferred_element_type=jnp.float32), "mp"
    )
    norm_two, second_pull = jax.vjp(layer_norm, first_sum)
    grad_gain_two = jnp.sum(grad_normed_two * norm_two, 0)
    grad_first = grad_second + second_pull(grad_normed_two * text_gain_two)[0]
    local_heads = text_qkv.shape[2] // HEAD
    grad_att_in = grad_first.astype(jnp.bfloat16)
    grad_out = jnp.einsum("rf,rd->fd", mixed_rows, grad_att_in, preferred_element_type=jnp.float32)
    grad_mixed = jnp.einsum("rd,fd->rf", grad_att_in, text_out, preferred_element_type=jnp.float32)
    grad_mixed = grad_mixed.astype(jnp.bfloat16).reshape(pair_count, length, local_heads, HEAD)
    scores = jnp.einsum(
        "nqhe,nkhe->nhqk", queries, key_rows, preferred_element_type=jnp.float32
    ) * HEAD ** (-0.5)
    scores = jnp.where(valid_keys[:, None, None, :], scores, -1000000000.0)
    softmax_rows = jnp.exp(scores - log_total)
    grad_values = jnp.einsum(
        "nhqk,nqhe->nkhe",
        softmax_rows.astype(jnp.bfloat16),
        grad_mixed,
        preferred_element_type=jnp.float32,
    ).astype(jnp.bfloat16)
    grad_soft = jnp.einsum(
        "nqhe,nkhe->nhqk", grad_mixed, value_rows, preferred_element_type=jnp.float32
    )
    grad_scores = (
        softmax_rows * (grad_soft - jnp.sum(grad_soft * softmax_rows, -1, keepdims=True))
    ).astype(jnp.bfloat16)
    grad_queries = (
        jnp.einsum("nhqk,nkhe->nqhe", grad_scores, key_rows, preferred_element_type=jnp.float32)
        * HEAD ** (-0.5)
    ).astype(jnp.bfloat16)
    grad_keys = (
        jnp.einsum("nhqk,nqhe->nkhe", grad_scores, queries, preferred_element_type=jnp.float32)
        * HEAD ** (-0.5)
    ).astype(jnp.bfloat16)
    stacked = jnp.stack([grad_queries, grad_keys, grad_values], 2).reshape(
        pair_count * length, 3, local_heads * HEAD
    )
    grad_qkv = jnp.einsum("rd,rcf->dcf", normed, stacked, preferred_element_type=jnp.float32)
    grad_normed = lax.psum(
        jnp.einsum("rcf,dcf->rd", stacked, text_qkv, preferred_element_type=jnp.float32), "mp"
    )
    flat_input = text_hidden.reshape(pair_count * length, model_width)
    norm_one, first_pull = jax.vjp(layer_norm, flat_input)
    grad_gain_one = jnp.sum(grad_normed * norm_one, 0)
    grad_rows = grad_first + first_pull(grad_normed * text_gain_one)[0]
    gain_half = model_width // lax.axis_size("mp")
    gain_one_part = lax.dynamic_slice_in_dim(grad_gain_one, mp_index * gain_half, gain_half, 0)
    gain_two_part = lax.dynamic_slice_in_dim(grad_gain_two, mp_index * gain_half, gain_half, 0)
    summed = lax.psum(
        (gain_one_part, gain_two_part, grad_qkv, grad_out, grad_up, grad_down, grad_proj), "batch"
    )
    return (
        loss,
        grad_rows.reshape(pair_count, length, model_width),
        summed[0],
        summed[1],
        summed[2],
        summed[3],
        summed[4],
        summed[5],
        summed[6],
        grad_log_temp,
    )


def solution(mesh):
    return jax.shard_map(
        per_device,
        mesh=mesh,
        in_specs=(
            P("batch", None, None),
            P("batch", None, None),
            P("batch", None),
            P(None, None, "mp"),
            P("mp", None),
            P(None, "mp"),
            P("mp", None),
            P(),
            P(),
            P(None, None, "mp"),
            P("mp", None),
            P(None, "mp"),
            P("mp", None),
            P(None, "mp"),
            P(),
        ),
        out_specs=(
            P(),
            P("batch", None, None),
            P("mp"),
            P("mp"),
            P(None, None, "mp"),
            P("mp", None),
            P(None, "mp"),
            P("mp", None),
            P(None, "mp"),
            P(),
        ),
        check_vma=False,
    )
```

profile of v0, /device:TPU:0, one launch (start us, length us, event | category | flops | bytes accessed | tf_op | source)
XLA Modules:
  0.0 779.0 jit_solution(17772054685410387118)
XLA Ops:
  7.2 1.2 convert_reduce_fusion.1
  8.6 1.1 fusion.50
  9.7 1.2 convert_reduce_fusion
  11.2 2.3 copy.82
  13.9 2.5 reshape.233
  16.4 2.9 convolution_convert_fusion
  19.3 2.7 reshape.234
  22.0 3.2 fusion.120
  25.2 2.6 fusion.123
  27.9 2.7 convolution_multiply_fusion
  32.0 2.6 convolution_convert_fusion.2
  34.7 1.5 reshape.230
  38.3 3.5 fusion.13
  41.8 2.1 copy.90
  44.0 1.8 reshape.235
  45.7 2.1 fusion.125
  47.9 2.6 fusion.127
  50.7 23.2 %all-reduce.19.cloned.1.call-done = (f32[128,768]{1,0:T(8,128)}, f32[400,768]{1,0:T(8,128)}) async-done(((f32[128,768]{1,0:T(8,128)}, f32[400,768]{1,0:T(8,128)}), (f32[128,768]{1,0:T(8,128)}, f32[400,768]{1,0:T(8,128)})) %all-reduce.19.cloned.1.call-update) | async-done | bytes 1622032 | tf_op jit(solution)/shard_map/psum | solution.py:66
  73.9 1.1 fusion.119
  75.7 1.9 fusion.117
  77.9 3.0 multiply_convert_fusion.2
  81.8 1.2 fusion.126
  83.0 10.7 %fusion.14 = f32[400,768]{1,0:T(8,128)} fusion(bf16[1536,768]{1,0:T(8,128)(2,1)} %param.21, bf16[768,1536]{1,0:T(8,128)(2,1)} %param.20, f32[400,768]{1,0:T(8,128)} %copy-done.1, f32[400]{0:T(512)S(1)} %add_rsqrt_fusion.1, f32[400]{0:T(512)S(1)} %broadcast_multiply_fusion.4), kind=kOutput, calls=%fused_computation.31 | convolution fusion | flops 1928294400 | bytes 7179392 | tf_op jit(solution)/shard_map/dot_general | solution.py:71
  95.8 1.2 dynamic-slice
  97.7 1.4 log_add_fusion
  99.1 16.4 %all-reduce.17.cloned.1.call-done = (f32[128,768]{1,0:T(8,128)}, f32[400,768]{1,0:T(8,128)}) async-done(((f32[128,768]{1,0:T(8,128)}, f32[400,768]{1,0:T(8,128)}), (f32[128,768]{1,0:T(8,128)}, f32[400,768]{1,0:T(8,128)})) %all-reduce.17.cloned.1.call-update) | async-done | bytes 1622032 | tf_op jit(solution)/shard_map/psum | solution.py:75
  115.6 2.9 add.159
  118.9 1.9 all_gather.13
  121.5 2.5 reshape.236
  124.0 2.1 reduce_sum.314
  126.9 1.4 multiply_reduce_fusion.8
  128.4 43.2 %all_gather.14 = f32[128,768]{1,0:T(8,128)S(1)} all-gather(f32[8,768]{1,0:T(8,128)S(1)} %get-tuple-element.30), channel_id=1, replica_groups=mesh['batch'=16,'mp'=2] {'batch'}, dimensions={0}, use_global_device_ids=true | all-gather | bytes 417792 | tf_op jit(solution)/shard_map/all_gather | solution.py:165
  171.6 37.7 %all_gather.15 = f32[128,768]{1,0:T(8,128)S(1)} all-gather(f32[8,768]{1,0:T(8,128)S(1)} %get-tuple-element.31), channel_id=1, replica_groups=mesh['batch'=16,'mp'=2] {'batch'}, dimensions={0}, use_global_device_ids=true | all-gather | bytes 417792 | tf_op jit(solution)/shard_map/all_gather | solution.py:166
  212.7 39.4 %all-reduce = f32[128]{0:T(128)} all-reduce(f32[128]{0:T(128)} %copy-done.55), channel_id=1, replica_groups=mesh['batch'=16,'mp'=2] {'batch'}, use_global_device_ids=true, to_apply=%add | all-reduce | flops 128 | bytes 1024
  252.1 1.4 multiply_reduce_fusion.7
  255.0 2.0 fusion.128
  256.9 4.6 psum.117
  262.4 4.1 fusion.131
  266.6 1.0 add_convert_fusion
  268.3 1.6 fusion.129
  270.0 2.2 fusion.110
  272.2 4.1 fusion.113
  276.3 8.4 %all-reduce.11.cloned.1.call-done = f32[128,768]{1,0:T(8,128)} async-done(((f32[128,768]{1,0:T(8,128)}), f32[128,768]{1,0:T(8,128)}) %all-reduce.11.cloned.1.call-update) | async-done | bytes 393232 | tf_op jit(solution)/shard_map/psum | solution.py:220
  284.7 1.3 multiply_reduce_fusion.2
  286.6 1.2 fusion.115
  290.7 1.3 multiply_reduce_fusion.3
  292.1 1.9 fusion.20
  294.1 0.9 fusion.21
  296.2 1.0 copy.94
  299.3 0.9 constant_dynamic-update-slice_fusion.1
  300.2 2.9 convolution_bitcast_fusion
  303.2 1.4 fusion.130
  304.5 2.4 fusion.55
  309.8 13.1 %all-reduce.13.cloned.1.call-done = f32[128,768]{1,0:T(8,128)} async-done(((f32[128,768]{1,0:T(8,128)}), f32[128,768]{1,0:T(8,128)}) %all-reduce.13.cloned.1.call-update) | async-done | bytes 393232 | tf_op jit(solution)/shard_map/psum | solution.py:260
  323.0 1.2 fusion.48
  324.2 1.3 fusion.47
  325.5 45.2 %all-reduce.1 = (f32[]{:T(128)}, f32[384]{0:T(512)}, f32[384]{0:T(512)}, f32[]{:T(128)}) all-reduce(f32[]{:T(128)S(6)} %sub.140, f32[384]{0:T(512)S(1)} %dynamic_slice.10, f32[384]{0:T(512)S(1)} %dynamic_slice.11, f32[]{:T(128)} %multiply_reduce_fusion.11), channel_id=1, replica_groups=mesh['batch'=16,'mp'=2] {'batch'}, use_global_device_ids=true, to_apply=%region_28.29 | all-reduce | flops 770 | bytes 6160 | tf_op jit(solution)/shard_map/psum | solution.py:196
  372.1 2.0 add_add_fusion.2
  374.1 384.4 %all-reduce.15.cloned.1.call-done = (f32[768,3,384]{2,0,1:T(8,128)}, f32[384,768]{1,0:T(8,128)}, f32[768,1536]{1,0:T(8,128)}, f32[1536,768]{1,0:T(8,128)}, f32[768,384]{1,0:T(8,128)}) async-done(((f32[768,3,384]{2,0,1:T(8,128)}, f32[384,768]{1,0:T(8,128)}, f32[768,1536]{1,0:T(8,128)}, f32[1536,768]{1,0:T(8,128)}, f32[768,384]{1,0:T(8,128)}), (f32[768,3,384]{2,0,1:T(8,128)}, f32[384,768]{1,0:T(8,128)}, ...) | async-done | bytes 15335440 | tf_op jit(solution)/shard_map/psum | solution.py:270
  758.4 4.2 copy.159
  762.6 1.0 copy.160
  763.6 2.4 copy.161
  767.1 2.2 copy.162
  769.2 1.0 copy.163
  (202 shorter events, 24.9 us)
Async XLA Ops:
  7.2 70.7 %copy-start = (bf16[768,1536]{1,0:T(8,128)(2,1)S(1)}, bf16[768,1536]{1,0:T(8,128)(2,1)}, u32[]{:S(2)}) copy-start(bf16[768,1536]{1,0:T(8,128)(2,1)} %param.26) | copy-start | bytes 7077892
  7.2 6.3 copy-start.3
  7.2 66.6 %all-reduce.19.cloned.1.call-start = ((), (), s32[]{:S(2)}) async-start(), calls=%async_computation.4 | async-start | bytes 3244032 | tf_op jit(solution)/shard_map/psum | solution.py:66
  8.6 22.7 %copy-start.34 = (f32[128]{0:T(128)}, f32[128]{0:T(128)S(1)}, u32[]{:S(2)}) copy-start(f32[128]{0:T(128)S(1)} %div.110) | copy-start | bytes 1540
  25.2 5.4 copy-start.31
  25.2 6.7 copy-start.2
  25.2 6.7 copy-start.30
  30.7 0.6 copy-start.52
  31.3 0.6 copy-start.40
  36.3 0.7 copy-start.17
  36.3 1.0 copy-start.18
  36.4 1.0 copy-start.20
  36.4 1.9 copy-start.58
  36.6 0.7 copy-start.28
  36.8 0.6 copy-start.29
  50.5 65.1 %all-reduce.17.cloned.1.call-start = ((), (), s32[]{:S(2)}) async-start(), calls=%async_computation.3 | async-start | bytes 3244032 | tf_op jit(solution)/shard_map/psum | solution.py:75
  75.0 2.9 copy-start.39
  75.2 0.5 copy-start.51
  75.7 2.2 copy-start.44
  75.7 2.2 copy-start.32
  77.6 3.4 copy-start.1
  77.9 3.8 copy-start.8
  81.0 0.8 copy-start.12
  93.7 191.0 %all-reduce.11.cloned.1.call-start = ((), (), s32[]{:S(2)}) async-start(), calls=%async_computation | async-start | bytes 786432 | tf_op jit(solution)/shard_map/psum | solution.py:220
  95.2 23.5 %copy-start.38 = (f32[8]{0:T(128)S(1)}, f32[8]{0:T(128)}, u32[]{:S(2)}) copy-start(f32[8]{0:T(128)} %copy-done.37) | copy-start | bytes 100
  97.7 154.4 %copy-start.48 = (s32[8]{0:T(128)}, s32[8]{0:T(128)S(1)}, u32[]{:S(2)}) copy-start(s32[8]{0:T(128)S(1)} %iota_add_fusion) | copy-start | bytes 100
  115.6 2.9 copy-start.26
  115.6 3.1 copy-start.10
  118.7 2.8 copy-start.27
  120.7 0.6 copy-start.24
  121.5 4.6 copy-start.54
  121.5 50.1 %copy-start.47 = (f32[8]{0:T(128)}, f32[8]{0:T(128)S(1)}, u32[]{:S(2)}) copy-start(f32[8]{0:T(128)S(1)} %add_rsqrt_fusion.2) | copy-start | bytes 100
  171.6 37.7 %copy-start.5 = (f32[128,768]{1,0:T(8,128)}, f32[128,768]{1,0:T(8,128)S(1)}, u32[]{:S(2)}) copy-start(f32[128,768]{1,0:T(8,128)S(1)} %all_gather.14) | copy-start | bytes 1179652
  210.6 43.6 %copy-start.42 = (f32[8]{0:T(128)}, f32[8]{0:T(128)S(1)}, u32[]{:S(2)}) copy-start(f32[8]{0:T(128)S(1)} %get-tuple-element.33) | copy-start | bytes 100
  262.4 4.2 copy-start.9
  262.4 4.2 copy-start.56
  262.4 4.2 copy-start.57
  267.6 0.7 copy-start.13
  270.0 53.0 %all-reduce.13.cloned.1.call-start = ((), (), s32[]{:S(2)}) async-start(), calls=%async_computation.1 | async-start | bytes 786432 | tf_op jit(solution)/shard_map/psum | solution.py:260
  272.2 12.5 %copy-start.33 = (f32[768]{0:T(1024)S(1)}, f32[768]{0:T(1024)}, u32[]{:S(2)}) copy-start(f32[768]{0:T(1024)} %param.23) | copy-start | bytes 9220
  284.7 4.8 copy-start.11
  287.9 0.8 copy-start.6
  287.9 4.2 copy-start.23
  287.9 6.2 copy-start.45
  290.7 3.4 copy-start.21
  290.7 4.3 copy-start.19
  294.1 4.0 copy-start.22
  296.2 7.0 copy-start.16
  303.1 455.3 %all-reduce.15.cloned.1.call-start = ((), (), s32[]{:S(2)}) async-start(), calls=%async_computation.2 | async-start | bytes 30670848 | tf_op jit(solution)/shard_map/psum | solution.py:270
  307.0 2.1 copy-start.43
  307.0 2.1 copy-start.49
  307.0 2.1 copy-start.50
  307.0 16.0 %copy-start.35 = (f32[128]{0:T(128)S(1)}, f32[128]{0:T(128)}, u32[]{:S(2)}) copy-start(f32[128]{0:T(128)} %copy-done.34) | copy-start | bytes 1540
  307.0 17.2 %copy-start.53 = (f32[128]{0:T(128)S(1)}, f32[128]{0:T(128)}, u32[]{:S(2)}) copy-start(f32[128]{0:T(128)} %copy-done.52) | copy-start | bytes 1540
  307.0 17.2 %copy-start.41 = (f32[128]{0:T(128)S(1)}, f32[128]{0:T(128)}, u32[]{:S(2)}) copy-start(f32[128]{0:T(128)} %copy-done.40) | copy-start | bytes 1540
  307.0 65.1 %copy-start.7 = (f32[128,768]{1,0:T(8,128)S(1)}, f32[128,768]{1,0:T(8,128)}, u32[]{:S(2)}) copy-start(f32[128,768]{1,0:T(8,128)} %copy-done.6) | copy-start | bytes 1179652
  307.0 65.1 %copy-start.25 = (f32[8,768]{1,0:T(8,128)S(1)}, f32[8,768]{1,0:T(8,128)}, u32[]{:S(2)}) copy-start(f32[8,768]{1,0:T(8,128)} %psum.117) | copy-start | bytes 73732
  307.0 65.1 %copy-start.36 = (f32[128]{0:T(128)S(1)}, f32[128]{0:T(128)}, u32[]{:S(2)}) copy-start(f32[128]{0:T(128)} %mul.379) | copy-start | bytes 1540
  307.0 65.1 %copy-start.46 = (f32[128]{0:T(128)S(1)}, f32[128]{0:T(128)}, u32[]{:S(2)}) copy-start(f32[128]{0:T(128)} %copy-done.45) | copy-start | bytes 1540
  758.4 4.2 copy-start.15
  758.4 5.2 copy-start.4
  762.6 4.2 slice-start
  763.6 3.4 slice-start.1
  767.1 2.2 copy-start.14
  (2 other events, 1.0 us)
Sparse Core Ops, SparseCore 0:
  50.6 23.2 all-reduce.18
  93.8 21.7 all-reduce.16
  270.1 14.5 all-reduce.10
  303.2 19.6 all-reduce.12
  330.4 428.0 all-reduce.14
where the time goes:
time: 781 us; the launch traced here: 779 us
  waiting for transfers between devices  446 us (57%)
  blocking collectives  172 us (22%)
  matrix products  63.6 us (8%)
  local copies, waits for them, and re-layouts  46 us (6%)
  other arithmetic  30.1 us (4%)
  between operations  21.4 us (3%)
    psum x1, waiting for transfers between devices, per_device(): lax.psum((gain_one_part, gain_two_part, grad_qkv, grad_out, grad_up, grad...  384 us
    psum x1, blocking collectives, per_device(): loss_sum, temp_sum = lax.psum((loss_part, temp_part), 'batch')  45.2 us
    all_gather x1, blocking collectives, per_device(): image_piece = lax.all_gather(image_norm, 'batch', axis=0, tiled=True)  43.2 us
    unnamed x1, blocking collectives  39.4 us
    all_gather x1, blocking collectives, per_device(): text_piece = lax.all_gather(text_norm, 'batch', axis=0, tiled=True)  37.7 us
    psum x1, waiting for transfers between devices, block_forward(): attended = lax.psum(partial_out, 'mp')  23.2 us
    unnamed x131, local copies, waits for them, and re-layouts  20.9 us
    psum x1, waiting for transfers between devices, block_forward(): downward = lax.psum(partial_down, 'mp')  16.4 us
  transfers between devices with their start and end apart: 5, of which 5 were waited for; matrix products, arithmetic and copies ran while one was open for 2% of the time, Pallas kernels for 0%

commit v1 on v0

v1 whole, which is shorter than its diff:
```python
import functools
import jax
import jax.numpy as jnp
from jax import lax
from jax.experimental import pallas as pl
from jax.experimental.pallas import tpu as pltpu
from jax.sharding import PartitionSpec as P

HEAD = 64
LN_EPS = 1e-06
NORM_EPS = 1e-06
HIGHEST = lax.Precision.HIGHEST
BF = jnp.bfloat16
F32 = jnp.float32
MIB = 2**20


def nn(a, b):
    return lax.dot_general(a, b, (((1,), (0,)), ((), ())), preferred_element_type=F32)


def nt(a, b):
    return lax.dot_general(a, b, (((1,), (1,)), ((), ())), preferred_element_type=F32)


def tn(a, b):
    return lax.dot_general(a, b, (((0,), (0,)), ((), ())), preferred_element_type=F32)


def normalize(rows):
    center = rows - jnp.mean(rows, -1, keepdims=True)
    inv = lax.rsqrt(jnp.mean(center * center, -1, keepdims=True) + LN_EPS)
    return center * inv, inv


def normalize_pull(grad, xhat, inv):
    return inv * (
        grad - jnp.mean(grad, -1, keepdims=True) - xhat * jnp.mean(grad * xhat, -1, keepdims=True)
    )


def two_heads(tile):
    first = lax.broadcasted_iota(jnp.int32, tile.shape, 1) < HEAD
    zero = jnp.zeros_like(tile)
    return jnp.concatenate([jnp.where(first, tile, zero), jnp.where(first, zero, tile)], 0)


def stack_heads(pair):
    half = pair.shape[1] // 2
    return jnp.concatenate([pair[:, :half], pair[:, half:]], 0)


def halves(values):
    high = values.astype(BF)
    return high, (values - high.astype(F32)).astype(BF)


SENTINEL = 1e30
SUB = 128
INSIDE = 128
CHUNK = 256


def text_kernel(
    x_ref, g1_ref, g2_ref, dmw_ref, dh_ref, qkv_h, out_h, up_h, oqkv_h, oout_h, oup_h,
    a1_ref, dqkv_ref, o_ref, dattn_ref, a2_ref, du_ref, gsum_ref, gain2_ref, rows_ref,
    qkv_s, p_s, h1_s, do_s, wqkv_ref, wout_ref, wup_ref, load_sem,
):
    step = pl.program_id(0)
    width = x_ref.shape[1]
    hidden = wup_ref.shape[1]
    pairs = gsum_ref.shape[0]
    g1 = g1_ref[...]
    g2 = g2_ref[...]
    half = width // 2
    tiles = half // 128
    length = SUB // 8

    def loads():
        pieces = []
        for g, h in enumerate((qkv_h, oqkv_h)):
            for k in range(3):
                at = (3 * g + k) * half
                pieces.append((h.at[k], wqkv_ref.at[:, at:at + half]))
        pieces += [(out_h, wout_ref.at[:half]), (oout_h, wout_ref.at[half:])]
        pieces += [(up_h, wup_ref.at[:, :hidden // 2]), (oup_h, wup_ref.at[:, hidden // 2:])]
        return [pltpu.make_async_copy(h, v, load_sem.at[i]) for i, (h, v) in enumerate(pieces)]

    @pl.when(step == 0)
    def _():
        for c in loads():
            c.start()

    x = x_ref[...]
    lane = lax.broadcasted_iota(jnp.int32, (CHUNK, 128), 0) + step * CHUNK
    idcol = jnp.where(x[:, :128] < 0.5 * SENTINEL, (lane // length).astype(F32), -1.0)
    x = jnp.where(x < 0.5 * SENTINEL, x, 0.0)
    xhat, _ = normalize(x)
    a1_ref[...] = (xhat * g1).astype(BF)

    @pl.when(step == 0)
    def _():
        for c in loads():
            c.wait()

    qkv_s[...] = nn(a1_ref[...], wqkv_ref[...]).astype(BF)
    masks = []
    for s in range(CHUNK // SUB):
        ids = idcol[s * SUB:(s + 1) * SUB, :]
        m = ids == ids.T
        masks.append((ids, ids.T, jnp.concatenate([m, m], 1)))

    def columns(group, kind, t):
        start = group * (3 * width // 2) + kind * (width // 2) + t * 128
        return slice(start, start + 128)

    for s in range(CHUNK // SUB):
        rows = slice(s * SUB, (s + 1) * SUB)
        for g in range(2):
            for t in range(tiles):
                q2 = qkv_s[rows, columns(g, 0, t)]
                k2 = qkv_s[rows, columns(g, 1, t)]
                v2 = qkv_s[rows, columns(g, 2, t)]
                st = nt(k2, two_heads(q2)) * HEAD ** (-0.5)
                st = jnp.where(masks[s][2], st, -1000000000.0)
                e = jnp.exp(st - jnp.max(st, 0, keepdims=True))
                p = e * (1.0 / jnp.sum(e, 0, keepdims=True))
                p_s[(s * 2 + g) * tiles + t] = p
                o = tn(stack_heads(p.astype(BF)), two_heads(v2))
                at = g * (width // 2) + t * 128
                o_ref[rows, at:at + 128] = o.astype(BF)
    h1 = x + nn(o_ref[...], wout_ref[...])
    h1_s[...] = h1
    xhat2, inv2 = normalize(h1)
    a2_ref[...] = (xhat2 * g2).astype(BF)

    lanes = lax.broadcasted_iota(jnp.int32, (CHUNK, 2 * pairs), 1)
    lanes = jnp.where(lanes < pairs, lanes, lanes - pairs).astype(F32)
    spread = (jnp.broadcast_to(idcol[:, :1], lanes.shape) == lanes).astype(BF)
    idrow = jnp.concatenate([m[1][:1] for m in masks], 1)
    subl = lax.broadcasted_iota(jnp.int32, (pairs, CHUNK), 0).astype(F32)
    gather = (jnp.broadcast_to(idrow, subl.shape) == subl).astype(BF)

    @pl.when(step == 0)
    def _():
        gsum_ref[...] = jnp.zeros_like(gsum_ref)
        gain2_ref[...] = jnp.zeros_like(gain2_ref)

    piece = 512
    da2 = None
    for j in range(hidden // piece):
        cols = slice(j * piece, (j + 1) * piece)
        u = nn(a2_ref[...], wup_ref[:, cols])
        cdf = 0.5 + 0.5 * lax.erf(u * 0.5 ** 0.5)
        g = (u * cdf).astype(BF)
        slope = cdf + u * (jnp.exp(-0.5 * u * u) * 0.3989422804014327)
        gsum_ref[:, cols] += nn(gather, g)
        du = (nn(spread, dmw_ref[:, cols]) * slope).astype(BF)
        du_ref[:, cols] = du
        part = nt(du, wup_ref[:, cols])
        da2 = part if da2 is None else da2 + part
    xhat2, inv2 = normalize(h1_s[...])
    gain2_ref[...] += jnp.sum(da2 * xhat2, 0, keepdims=True)
    dh1 = nn(spread, dh_ref[...]) + normalize_pull(da2 * g2, xhat2, inv2)
    dattn_ref[...] = dh1.astype(BF)
    do_s[...] = nt(dattn_ref[...], wout_ref[...]).astype(BF)

    for s in range(CHUNK // SUB):
        rows = slice(s * SUB, (s + 1) * SUB)
        for g in range(2):
            for t in range(tiles):
                q2 = qkv_s[rows, columns(g, 0, t)]
                k2 = qkv_s[rows, columns(g, 1, t)]
                v2 = qkv_s[rows, columns(g, 2, t)]
                at = g * (width // 2) + t * 128
                do2 = two_heads(do_s[rows, at:at + 128])
                dp = nt(v2, do2)
                p = p_s[(s * 2 + g) * tiles + t]
                ds = (p * (dp - jnp.sum(dp * p, 0, keepdims=True))).astype(BF)
                dqkv_ref[rows, columns(g, 2, t)] = nn(p.astype(BF), do2).astype(BF)
                dqkv_ref[rows, columns(g, 1, t)] = (
                    nn(ds, two_heads(q2)) * HEAD ** (-0.5)
                ).astype(BF)
                dqkv_ref[rows, columns(g, 0, t)] = (
                    tn(stack_heads(ds), two_heads(k2)) * HEAD ** (-0.5)
                ).astype(BF)

    @pl.when(step == 0)
    def _():
        own = rows_ref.shape[0]
        da1 = nt(dqkv_ref[:own, :], wqkv_ref[...])
        xhat, inv = normalize(x[:own])
        rows_ref[...] = dh1[:own] + normalize_pull(da1 * g1, xhat, inv)


def text_pass(x, group, g1, g2, dmw, dh, weights, own):
    width = x.shape[1]
    pairs = dh.shape[0] // 2
    hidden = dmw.shape[1]
    total = pairs * own[1]
    steps = total // CHUNK
    whole = lambda a: pl.BlockSpec(a.shape, lambda i: (0,) * len(a.shape), pipeline_mode=pl.Buffered(1))
    fixed = lambda *shape: pl.BlockSpec(shape, lambda i: (0,) * len(shape))
    block = lambda cols: pl.BlockSpec((CHUNK, cols), lambda i: (i, 0))
    hbm = pl.BlockSpec(memory_space=pl.ANY)
    tiles = width // 128
    shape = jax.ShapeDtypeStruct
    return pl.pallas_call(
        text_kernel,
        grid=(steps,),
        out_shape=(
            shape((total, width), BF), shape((total, 3 * width), BF), shape((total, width), BF),
            shape((total, width), BF), shape((total, width), BF), shape((total, hidden), BF),
            shape((pairs, hidden), F32), shape((1, width), F32), shape((own[0], width), F32),
        ),
        in_specs=[
            pl.BlockSpec((CHUNK, width), lambda i: (i + group * steps, 0)), whole(g1), whole(g2), whole(dmw), whole(dh),
        ] + [hbm] * 6,
        out_specs=(
            block(width), block(3 * width), block(width), block(width), block(width), block(hidden),
            fixed(pairs, hidden), fixed(1, width), fixed(own[0], width),
        ),
        scratch_shapes=[
            pltpu.VMEM((CHUNK, 3 * width), BF),
            pltpu.VMEM((CHUNK // SUB * tiles, SUB, 2 * SUB), F32),
            pltpu.VMEM((CHUNK, width), F32),
            pltpu.VMEM((CHUNK, width), BF),
            pltpu.VMEM((width, 3 * width), BF),
            pltpu.VMEM((width, width), BF),
            pltpu.VMEM((width, hidden), BF),
            pltpu.SemaphoreType.DMA((10,)),
        ],
        compiler_params=pltpu.CompilerParams(vmem_limit_bytes=56 * MIB),
        name="text_pass",
    )(x, g1, g2, dmw, dh, *weights)


def weight_kernel(a_ref, g_ref, *refs):
    refs[-1][...] = tn(a_ref[...], g_ref[...]) if len(refs) == 1 else refs[0][...] + tn(a_ref[...], g_ref[...])


def weight_grad(a, a_at, a_cols, g, g_at, g_cols, tile, name, init=None):
    total = a.shape[0]
    out_spec = pl.BlockSpec((a_cols, tile), lambda i: (0, i))
    return pl.pallas_call(
        weight_kernel,
        grid=(g_cols // tile,),
        out_shape=jax.ShapeDtypeStruct((a_cols, g_cols), F32),
        in_specs=[
            pl.BlockSpec((total, a_cols), lambda i: (0, a_at // a_cols)),
            pl.BlockSpec((total, tile), lambda i: (0, g_at // tile + i)),
        ] + ([] if init is None else [out_spec]),
        out_specs=out_spec,
        input_output_aliases={} if init is None else {2: 0},
        compiler_params=pltpu.CompilerParams(vmem_limit_bytes=56 * MIB),
        name=name,
    )(a, g, *(() if init is None else (init,)))


MESH = pl.DeviceIdType.MESH


def chip_grid(mesh):
    chips = mesh.devices.reshape(-1, mesh.shape["mp"])[:, 0]
    places = [getattr(d, "coords", None) for d in chips]
    if all(p is not None and len(p) == 3 for p in places):
        grid = tuple(len({p[i] for p in places}) for i in (2, 1, 0))
        if grid[0] * grid[1] * grid[2] == len(chips):
            return grid
    side = 1
    while (2 * side) ** 3 <= len(chips):
        side *= 2
    return (len(chips) // (side * side), side, side)


class Spread:
    def __init__(self, grid, place, core, block, send, recv, first):
        self.grid, self.place, self.core = grid, place, core
        self.block, self.send, self.recv = block, send, recv
        self.first = first
        self.sent = []
        zs, ys, xs = grid
        self.turn = ys == xs
        near = []
        for d in range(1, zs // 2 + 1):
            near += [d] if 2 * d == zs else [d, zs - d]
        self.zorder = near
        self.aorder = list(range(1, ys))
        self.border = list(range(1, xs))
        self.pending = [("z", k) for k in near]
        self.pending += [("a", a, k) for a in self.aorder for k in [0] + near]

    def slot(self, kz, ka, kb):
        zs, ys, xs = self.grid
        plain = (kz * ys + ka) * xs + kb
        if not self.turn:
            return plain
        other = (kz * ys + kb) * xs + ka
        return plain if plain == other else plain + self.core * (other - plain)

    def target(self, dz, da, db):
        zs, ys, xs = self.grid
        z, y, x = self.place
        if self.turn and da != db:
            dy = da + self.core * (db - da)
            dx = db + self.core * (da - db)
        else:
            dy, dx = da, db
        batch = (lax.rem(z + dz, zs) * ys + lax.rem(y + dy, ys)) * xs + lax.rem(x + dx, xs)
        return (batch, self.core)

    def copy(self, source, landing, to):
        index = len(self.sent)
        sent = pltpu.make_async_remote_copy(
            src_ref=source, dst_ref=self.block(landing), send_sem=self.send.at[index],
            recv_sem=self.recv.at[landing], device_id=to, device_id_type=MESH,
        )
        sent.start()
        self.sent.append(sent)

    def along_a(self, source, kz):
        ys = self.grid[1]
        for d in self.aorder:
            self.copy(source, self.slot(kz, ys - d, 0), self.target(0, d, 0))

    def along_b(self, source, kz, ka):
        xs = self.grid[2]
        for d in self.border:
            self.copy(source, self.slot(kz, ka, xs - d), self.target(0, 0, d))

    def start(self):
        zs = self.grid[0]
        self.along_b(self.first, 0, 0)
        self.along_a(self.first, 0)
        for d in self.zorder:
            self.copy(self.first, self.slot(zs - d, 0, 0), self.target(d, 0, 0))

    def arrive(self, slot):
        pltpu.make_async_remote_copy(
            src_ref=self.block(slot), dst_ref=self.block(slot), send_sem=self.send.at[0],
            recv_sem=self.recv.at[slot], device_id=self.target(1, 0, 0), device_id_type=MESH,
        ).wait_recv()

    def serve(self, count=1):
        for _ in range(min(count, len(self.pending))):
            event = self.pending.pop(0)
            if event[0] == "z":
                slot = self.slot(event[1], 0, 0)
                self.arrive(slot)
                self.along_b(self.block(slot), event[1], 0)
                self.along_a(self.block(slot), event[1])
            else:
                slot = self.slot(event[2], event[1], 0)
                self.arrive(slot)
                self.along_b(self.block(slot), event[2], event[1])

    def finish(self):
        self.serve(len(self.pending))
        for a in [0] + self.aorder:
            for b in self.border:
                for k in [0] + self.zorder:
                    self.arrive(self.slot(k, a, b))
        for sent in self.sent:
            sent.wait_send()

    @staticmethod
    def copies(grid):
        zs, ys, xs = grid
        return (zs - 1) + zs * (ys - 1) + zs * ys * (xs - 1)


def attend(qkv_ref, o_ref, start, ids, half, both):
    m = ids == ids.T
    m = jnp.concatenate([m, m], 1)
    rows = pl.ds(start, SUB)
    for t in range(half // 128):
        q2 = qkv_ref[rows, t * 128:(t + 1) * 128]
        k2 = qkv_ref[rows, half + t * 128:half + (t + 1) * 128]
        v2 = qkv_ref[rows, 2 * half + t * 128:2 * half + (t + 1) * 128]
        st = nt(k2, two_heads(q2)) * HEAD ** (-0.5)
        st = jnp.where(m, st, -1000000000.0)
        e = jnp.exp(st - jnp.max(st, 0, keepdims=True))
        p = e * (1.0 / jnp.sum(e, 0, keepdims=True))
        o_ref[rows, t * 128:(t + 1) * 128] = tn(stack_heads(p.astype(BF)), two_heads(v2)).astype(BF)


def front_kernel(
    grid,
    rows_ref, mask_ref, image_ref, g1_ref, g2_ref, temp_ref,
    iqkv_h, iout_h, iup_h, idown_h, tqkv_h, tout_h, tup_h, tdown_h, tproj_h,
    xg_ref, oqkv_h, oout_h, oup_h, dmw_ref, dh_ref, dm_ref, low_ref, gh_ref, scal_ref,
    iqkv, iout, iup, idown, tqkv, tout, tup, tdown, proj,
    own_x, small, small_abs, payload, qkv_s, o_s, image_x, part, part_in, sums, sums_in,
    wsend_qkv, wsend_out, wsend_up, wsend_proj, wland_qkv, wland_out, wland_up, wland_proj,
    dmw_send, dmw_in, cos_s, tnorm_s,
    load_sem, out_sem, x_send, x_recv, s_send, s_recv, c_send, c_recv, own_sem,
):
    zs, ys, xs = grid
    chips = zs * ys * xs
    batch, core = lax.axis_index("batch"), lax.axis_index("mp")
    place = (batch // (ys * xs), lax.rem(batch // xs, ys), lax.rem(batch, xs))
    partner = (batch, 1 - core)
    pairs, length = mask_ref.shape
    rows = pairs * length
    width = rows_ref.shape[1]
    half = width // 2
    hidden = tup.shape[1]
    hp = pairs // 2
    hr = hp * length
    total = chips * pairs
    mine = chips * hp
    patches = image_ref.shape[0] // pairs
    padded = image_x.shape[0] // pairs

    inside = total <= INSIDE

    loads = []
    for i, (h, v) in enumerate((
        (tqkv_h, tqkv), (iqkv_h, iqkv), (iout_h, iout), (tout_h, tout), (tup_h, tup), (iup_h, iup), (idown_h, idown),
        (tdown_h, tdown), (tproj_h, proj.at[0]),
    )):
        v = v if h is not tproj_h else proj.at[core]
        loads.append(pltpu.make_async_copy(h, v, load_sem.at[i]))
        loads[-1].start()

    gather = Spread(grid, place, core, lambda s: xg_ref.at[s], x_send, x_recv, own_x)
    peers = [partner]
    peers += [gather.target(d, 0, 0) for d in range(1, zs)]
    peers += [gather.target(0, d, 0) for d in range(1, ys)]
    peers += [gather.target(0, 0, d) for d in range(1, xs)]
    barrier = pltpu.get_barrier_semaphore()
    for peer in peers:
        pl.semaphore_signal(barrier, inc=1, device_id=peer, device_id_type=MESH)

    mask = mask_ref[...].astype(F32)
    lane = lax.broadcasted_iota(jnp.int32, (rows, length), 1)
    sub = lax.broadcasted_iota(jnp.int32, (rows, length), 0)
    spread_mask = jnp.broadcast_to(mask[:, None, :], (pairs, length, length)).reshape(rows, length)
    valid = jnp.sum(jnp.where(lane == lax.rem(sub, length), spread_mask, 0.0), 1, keepdims=True)
    text_x = rows_ref[...].astype(F32)
    marked = jnp.where(valid > 0, text_x, SENTINEL)
    own_x[...] = jnp.where(core == 0, marked[:hr], marked[hr:])
    pl.semaphore_wait(barrier, len(peers))
    gather.start()
    own_copy = pltpu.make_async_copy(own_x, xg_ref.at[0], own_sem)
    own_copy.start()

    g1, g2 = g1_ref[...], g2_ref[...]
    a1 = (normalize(text_x)[0] * g1).astype(BF)
    loads[0].wait()
    for k in range(3):
        qkv_s[:rows, k * half:(k + 1) * half] = nn(a1, tqkv[k]).astype(BF)
    pair_of = (lax.broadcasted_iota(jnp.int32, (rows, 128), 0) // length).astype(F32)
    attend(qkv_s, o_s, 0, jnp.where(valid > 0, pair_of, -1.0), half, None)
    loads[3].wait()
    top = padded * pairs
    part[top:, :] = nn(o_s[:rows, :], tout[...])

    def swap(source, landing, index):
        c = pltpu.make_async_remote_copy(
            src_ref=source, dst_ref=landing, send_sem=c_send.at[index], recv_sem=c_recv.at[index],
            device_id=partner, device_id_type=MESH,
        )
        c.start()
        return c

    def contrast():
        for s in range(chips):
            kz, ky, kx = s // (ys * xs), s // xs % ys, s % xs
            at = (lax.rem(place[0] + kz, zs) * ys + lax.rem(place[1] + ky, ys)) * xs + lax.rem(place[2] + kx, xs)
            small_abs[:, at] = small[:, s]
        low = small_abs[0, :, :, :width].reshape(total, width).astype(BF)
        low_ref[...] = low
        counts = small_abs[0, :, :, width:].reshape(total, 128)[:, :1]
        embed = jnp.concatenate([nn(low, proj[0]), nn(low, proj[1])], 1)
        inv = lax.rsqrt(jnp.sum(embed * embed, 1, keepdims=True) + NORM_EPS)
        tnorm_s[...] = embed * inv
        images = small_abs[1, :, :, :width].reshape(total, width)
        scale = jnp.exp(jnp.full((1, 1), temp_ref[0, 0], F32))
        cos_s[...] = lax.dot_general(
            tnorm_s[...], images, (((1,), (1,)), ((), ())), precision=HIGHEST, preferred_element_type=F32
        )
        logits = cos_s[...] * scale
        row_top = jnp.max(logits, 1, keepdims=True)
        row_lse = row_top + jnp.log(jnp.sum(jnp.exp(logits - row_top), 1, keepdims=True))
        col_top = jnp.max(logits, 0, keepdims=True)
        col_lse = col_top + jnp.log(jnp.sum(jnp.exp(logits - col_top), 0, keepdims=True))
        eye = (lax.broadcasted_iota(jnp.int32, (total, total), 0) == lax.broadcasted_iota(jnp.int32, (total, total), 1))
        eye = eye.astype(F32)
        pair_grad = (jnp.exp(logits - row_lse) + jnp.exp(logits - col_lse) - 2.0 * eye) * (0.5 / total)

        def everything(v):
            return jnp.sum(jnp.sum(v, 1, keepdims=True), 0, keepdims=True)

        loss = (everything(row_lse) + everything(col_lse) - 2.0 * everything(logits * eye)) * (0.5 / total)
        temp = scale * everything(pair_grad * cos_s[...])
        lane = lax.broadcasted_iota(jnp.int32, (8, 128), 1)
        scal_ref[...] = jnp.where(lane == 0, loss, temp)
        grad_norm = scale * lax.dot_general(
            pair_grad, images, (((1,), (0,)), ((), ())), precision=HIGHEST, preferred_element_type=F32
        )
        tnorm = tnorm_s[...]
        grad_embed = ((grad_norm - tnorm * jnp.sum(tnorm * grad_norm, 1, keepdims=True)) * inv).astype(BF)
        gh_ref[...] = jnp.where(core == 0, grad_embed[:, :half], grad_embed[:, half:])
        dh = (nt(grad_embed[:, :half], proj[0]) + nt(grad_embed[:, half:], proj[1])) / counts
        dm = dh.astype(BF)

        r = lax.broadcasted_iota(jnp.int32, (total, total), 0)
        owner = jnp.where(r < mine, core, 1 - core)
        r = lax.rem(r, mine)
        k, i = r // hp, lax.rem(r, hp)
        at = (lax.rem(place[0] + k // (ys * xs), zs) * ys + lax.rem(place[1] + lax.rem(k // xs, ys), ys)) * xs
        at = at + lax.rem(place[2] + lax.rem(k, xs), xs)
        pick = (at * pairs + owner * hp + i == lax.broadcasted_iota(jnp.int32, (total, total), 1)).astype(BF)
        dm_sorted = nn(pick, dm).astype(BF)
        dm_ref[...] = dm_sorted
        dmw = nt(dm_sorted, tdown[...])
        dmw_send[...] = dmw[mine:]
        dmw_swap = swap(dmw_send, dmw_in, 8)
        dh_high, dh_low = halves(dh)
        dh_ref[:mine, :] = nn(pick[:mine], dh_high).astype(BF)
        dh_ref[mine:, :] = nn(pick[:mine], dh_low).astype(BF)
        dmw_high, dmw_low = halves(dmw[:mine])
        dmw_ref[:mine, :hidden] = dmw_high
        dmw_ref[mine:, :hidden] = dmw_low
        return dmw_swap

    swaps = []
    text_swap = swap(part.at[pl.ds(top, rows)], part_in.at[pl.ds(top, rows)], 0)
    swaps.append(text_swap)

    r = lax.broadcasted_iota(jnp.int32, (padded * pairs, patches * pairs), 0)
    c = lax.broadcasted_iota(jnp.int32, (padded * pairs, patches * pairs), 1)
    place_of = lax.rem(r, padded) * pairs + r // padded
    reorder = jnp.where((place_of == c) & (lax.rem(r, padded) < patches), 1.0, 0.0).astype(BF)
    image_x[...] = nn(reorder, image_ref[...])
    a1 = normalize(image_x[...])[0].astype(BF)
    loads[1].wait()
    for k in range(3):
        qkv_s[:, k * half:(k + 1) * half] = nn(a1, iqkv[k]).astype(BF)
    gather.serve(1)
    for s in range(padded * pairs // SUB):
        r = lax.broadcasted_iota(jnp.int32, (SUB, 128), 0) + s * SUB
        ids = jnp.where(lax.rem(r, padded) < patches, (r // padded).astype(F32), -1.0)
        attend(qkv_s, o_s, s * SUB, ids, half, None)
        if s % 2 == 1:
            gather.serve(1)
    loads[2].wait()
    part[:top, :] = nn(o_s[...], iout[...])
    image_swap = swap(part.at[pl.ds(0, top)], part_in.at[pl.ds(0, top)], 1)
    swaps.append(image_swap)
    gather.serve(1)

    for k in range(3):
        wsend_qkv[k] = tqkv[k].astype(F32)
    wsend_out[...] = tout[...].astype(F32)
    loads[4].wait()
    wsend_up[...] = tup[...].astype(F32)
    loads[8].wait()
    wsend_proj[...] = proj[core].astype(F32)

    text_swap.wait_recv()
    h1 = text_x + (part[top:, :] + part_in[top:, :])
    a2 = (normalize(h1)[0] * g2).astype(BF)
    mean_h = jnp.sum((h1 * valid).reshape(pairs, length, width), 1)
    piece = 512
    bars = []
    for j in range(hidden // piece):
        u = nn(a2, tup[:, j * piece:(j + 1) * piece])
        g = (u * (0.5 + 0.5 * lax.erf(u * 0.5 ** 0.5))).astype(BF).astype(F32) * valid
        bars.append(jnp.sum(g.reshape(pairs, length, piece), 1))
    bar = jnp.concatenate(halves(jnp.concatenate(bars, 1)), 0)
    loads[7].wait()
    low = nn(bar, tdown[...])
    text_sum = low[:pairs] + low[pairs:]
    sums[:pairs, :] = text_sum

    image_swap.wait_recv()
    proj_swap = swap(wsend_proj, wland_proj, 2)
    qkv_swap = swap(wsend_qkv, wland_qkv, 3)
    out_swap = swap(wsend_out, wland_out, 4)
    up_swap = swap(wsend_up, wland_up, 5)
    swaps += [proj_swap, qkv_swap, out_swap, up_swap]
    image_x[...] += part[:top, :] + part_in[:top, :]
    a2 = normalize(image_x[...])[0].astype(BF)
    mean_i = jnp.sum(image_x[...].reshape(pairs, padded, width), 1)
    loads[5].wait()
    bars = []
    for j in range(hidden // piece):
        u = nn(a2, iup[:, j * piece:(j + 1) * piece])
        g = (u * (0.5 + 0.5 * lax.erf(u * 0.5 ** 0.5))).astype(BF).astype(F32)
        bars.append(jnp.sum(g.reshape(pairs, padded, piece), 1))
        gather.serve(1)
    bar = jnp.concatenate(halves(jnp.concatenate(bars, 1)), 0)
    loads[6].wait()
    low = nn(bar, idown[...])
    sums[pairs:, :] = low[:pairs] + low[pairs:]
    sums_swap = swap(sums, sums_in, 6)
    swaps.append(sums_swap)
    gather.serve(1)
    sums_swap.wait_recv()
    count = jnp.sum(mask, 1, keepdims=True)
    pooled = (mean_h + (sums[:pairs, :] + sums_in[:pairs, :])) / count
    e = (mean_i + (sums[pairs:, :] + sums_in[pairs:, :])) * (1.0 / patches)
    image_norm = e * lax.rsqrt(jnp.sum(e * e, 1, keepdims=True) + NORM_EPS)
    payload[:, :width] = jnp.where(core == 0, pooled, image_norm)
    payload[:, width:] = jnp.broadcast_to(count, (pairs, 128))
    spread = Spread(grid, place, core, lambda s: small.at[core, s], s_send, s_recv, payload)
    spread.start()
    small[core, 0] = payload[...]
    gather.serve(1)
    spread.finish()
    both_swap = swap(small.at[core], small.at[core], 7)
    swaps.append(both_swap)
    gather.serve(len(gather.pending))
    both_swap.wait_recv()

    proj_swap.wait_recv()
    proj[1 - core] = wland_proj[...].astype(BF)
    if inside:
        dmw_swap = contrast()
        swaps.append(dmw_swap)
    else:
        dmw_ref[...] = small[...]
        dm_ref[...] = proj[...]

    oqkv, oout, oup = iqkv, iout, iup
    outs = []
    qkv_swap.wait_recv()
    for k in range(3):
        oqkv[k] = wland_qkv[k].astype(BF)
    outs.append(pltpu.make_async_copy(oqkv, oqkv_h, out_sem.at[0]))
    outs[-1].start()
    out_swap.wait_recv()
    oout[...] = wland_out[...].astype(BF)
    outs.append(pltpu.make_async_copy(oout, oout_h, out_sem.at[1]))
    outs[-1].start()
    up_swap.wait_recv()
    oup[...] = wland_up[...].astype(BF)
    outs.append(pltpu.make_async_copy(oup, oup_h, out_sem.at[2]))
    outs[-1].start()
    if inside:
        dmw_swap.wait_recv()
        dmw_high, dmw_low = halves(dmw_in[...])
        dmw_ref[:mine, hidden:] = dmw_high
        dmw_ref[mine:, hidden:] = dmw_low
    gather.finish()
    own_copy.wait()
    for s in swaps:
        s.wait_send()
    for o in outs:
        o.wait()


def front(grid, rows, mask, image, g1, g2, temp, weights):
    chips = grid[0] * grid[1] * grid[2]
    pairs, length = mask.shape
    width = rows.shape[1]
    half = width // 2
    iqkv, iout, iup, idown, tqkv, tout, tup, tdown, tproj = weights
    hidden = tup.shape[1]
    total = chips * pairs
    mine = total // 2
    patches = image.shape[0] // pairs
    padded = -(-patches // 64) * 64
    top = padded * pairs
    hr = pairs // 2 * length
    vmem = pl.BlockSpec(memory_space=pltpu.VMEM)
    hbm = pl.BlockSpec(memory_space=pl.ANY)
    shape = jax.ShapeDtypeStruct
    copies = Spread.copies(grid)
    inside = total <= INSIDE
    if inside:
        ends = (
            shape((2 * mine, 2 * hidden), BF), shape((2 * mine, width), BF), shape((total, width), BF),
            shape((total, width), BF), shape((total, half), BF), shape((8, 128), F32),
        )
    else:
        mine, total = 8, 128
        ends = (shape((2, chips, pairs, width + 128), F32),) + (shape((8, 128), F32),)
        ends += (shape((2,) + tproj.shape, BF),) + (shape((8, 128), F32),) * 3
    return pl.pallas_call(
        functools.partial(front_kernel, grid),
        out_shape=(
            shape((chips, hr, width), F32),
            shape(tqkv.shape, BF), shape(tout.shape, BF), shape(tup.shape, BF),
        ) + ends,
        in_specs=[vmem] * 5 + [pl.BlockSpec(memory_space=pltpu.SMEM)] + [hbm] * 9,
        out_specs=[hbm] * 4 + [vmem] * 6,
        scratch_shapes=[
            pltpu.VMEM(iqkv.shape, BF), pltpu.VMEM(iout.shape, BF), pltpu.VMEM(iup.shape, BF), pltpu.VMEM(idown.shape, BF),
            pltpu.VMEM(tqkv.shape, BF), pltpu.VMEM(tout.shape, BF), pltpu.VMEM(tup.shape, BF), pltpu.VMEM(tdown.shape, BF),
            pltpu.VMEM((2,) + tproj.shape, BF),
            pltpu.VMEM((hr, width), F32),
            pltpu.VMEM((2, chips, pairs, width + 128), F32),
            pltpu.VMEM((2, chips if inside else 1, pairs, width + 128), F32),
            pltpu.VMEM((pairs, width + 128), F32),
            pltpu.VMEM((top, 3 * half), BF),
            pltpu.VMEM((top, half), BF),
            pltpu.VMEM((top, width), F32),
            pltpu.VMEM((top + pairs * length, width), F32),
            pltpu.VMEM((top + pairs * length, width), F32),
            pltpu.VMEM((2 * pairs, width), F32),
            pltpu.VMEM((2 * pairs, width), F32),
            pltpu.VMEM(tqkv.shape, F32), pltpu.VMEM(tout.shape, F32), pltpu.VMEM(tup.shape, F32), pltpu.VMEM(tproj.shape, F32),
            pltpu.VMEM(tqkv.shape, F32), pltpu.VMEM(tout.shape, F32), pltpu.VMEM(tup.shape, F32), pltpu.VMEM(tproj.shape, F32),
            pltpu.VMEM((mine, hidden), F32), pltpu.VMEM((mine, hidden), F32),
            pltpu.VMEM((total, total), F32), pltpu.VMEM((total, width), F32),
            pltpu.SemaphoreType.DMA((9,)), pltpu.SemaphoreType.DMA((3,)),
            pltpu.SemaphoreType.DMA((copies,)), pltpu.SemaphoreType.DMA((chips,)),
            pltpu.SemaphoreType.DMA((copies,)), pltpu.SemaphoreType.DMA((chips,)),
            pltpu.SemaphoreType.DMA((9,)), pltpu.SemaphoreType.DMA((9,)), pltpu.SemaphoreType.DMA,
        ],
        compiler_params=pltpu.CompilerParams(collective_id=0, has_side_effects=True, vmem_limit_bytes=60 * MIB),
        name="front",
    )(rows, mask, image, g1, g2, temp, *weights)


def contrast_outside(grid, small, proj, log_temp, text_down):
    core = lax.axis_index("mp")
    here = lax.axis_index("batch")
    chips, pairs, width = small.shape[1], small.shape[2], small.shape[3] - 128
    half = width // 2
    zs, ys, xs = grid
    slots = jnp.arange(chips, dtype=jnp.int32)
    z, y, x = here // (ys * xs), here // xs % ys, here % xs
    offset = (z + slots // (ys * xs)) % zs * (ys * xs) + (y + slots // xs % ys) % ys * xs + (x + slots % xs) % xs
    slot_of = jnp.argsort(offset)
    ordered = small[:, slot_of].reshape(2, chips * pairs, width + 128)
    low = ordered[0, :, :width].astype(BF)
    counts = ordered[0, :, width:width + 1]
    images = ordered[1, :, :width]
    total = chips * pairs
    embed = jnp.concatenate([nn(low, proj[0]), nn(low, proj[1])], 1)
    inv = lax.rsqrt(jnp.sum(embed * embed, 1, keepdims=True) + NORM_EPS)
    text_norm = embed * inv
    scale = jnp.exp(log_temp)
    cosine = jnp.dot(text_norm, images.T, precision=HIGHEST, preferred_element_type=F32)
    logits = scale * cosine
    text_lse = jax.nn.logsumexp(logits, 1, keepdims=True)
    image_lse = jax.nn.logsumexp(logits, 0, keepdims=True)
    eye = jnp.eye(total, dtype=F32)
    pair_grad = (jnp.exp(logits - text_lse) + jnp.exp(logits - image_lse) - 2.0 * eye) / (2.0 * total)
    loss = (jnp.sum(text_lse) + jnp.sum(image_lse) - 2.0 * jnp.sum(logits * eye)) / (2.0 * total)
    temp = scale * jnp.sum(pair_grad * cosine)
    grad_norm = scale * jnp.dot(pair_grad, images, precision=HIGHEST, preferred_element_type=F32)
    grad_embed = ((grad_norm - text_norm * jnp.sum(text_norm * grad_norm, 1, keepdims=True)) * inv).astype(BF)
    grad_half = lax.dynamic_slice_in_dim(grad_embed, core * half, half, 1)
    dh = (nt(grad_embed[:, :half], proj[0]) + nt(grad_embed[:, half:], proj[1])) / counts
    hp = pairs // 2

    def mine(v, c):
        w = v.reshape(chips, 2, hp, v.shape[-1])[offset]
        return lax.dynamic_index_in_dim(w, c, 1, keepdims=False).reshape(total // 2, v.shape[-1])

    def grouped(v):
        high, rest = halves(v)
        size = INSIDE // 8
        both = jnp.stack([high.reshape(-1, size, v.shape[1]), rest.reshape(-1, size, v.shape[1])], 1)
        return both.reshape(-1, v.shape[1])

    dm = jnp.concatenate([mine(dh, core), mine(dh, 1 - core)], 0).astype(BF)
    dmw = nt(dm, text_down)
    dmw_other = lax.ppermute(dmw[total // 2:], "mp", [(0, 1), (1, 0)])
    dmw = grouped(jnp.concatenate([dmw[:total // 2], dmw_other], 1))
    return dmw, grouped(mine(dh, core)), dm, low, grad_half, jnp.stack([loss, temp]).reshape(1, 2)


def per_device(
    grid, image_patches, text_rows, text_mask, image_qkv, image_out, image_up, image_down, text_gain_one, text_gain_two,
    text_qkv, text_out, text_up, text_down, text_proj, log_temp,
):
    pair_count, length, width = text_rows.shape
    core = lax.axis_index("mp")
    swap = [(0, 1), (1, 0)]
    half = width // 2
    hidden = text_up.shape[1]
    patches = jnp.transpose(image_patches, (1, 0, 2)).reshape(-1, width)
    iqkv = jnp.transpose(image_qkv, (1, 0, 2))
    tqkv = jnp.transpose(text_qkv, (1, 0, 2))
    g1, g2 = text_gain_one[None], text_gain_two[None]
    xg, oqkv, oout, oup, dmw, dh, dm, low, grad_half, scal = front(
        grid, text_rows.reshape(-1, width), text_mask, patches, g1, g2, log_temp.reshape(1, 1),
        (iqkv, image_out, image_up, image_down, tqkv, text_out, text_up, text_down, text_proj),
    )
    own = pair_count // 2 * length
    if dm.ndim == 3:
        dmw, dh, dm, low, grad_half, scal = contrast_outside(grid, dmw, dm, log_temp, text_down)
    rows_x = xg.reshape(-1, width)
    group_pairs = dm.shape[0] // 2 if dm.shape[0] <= INSIDE else INSIDE // 8

    def group(x, dmw, dh, init):
        a1, dqkv, o, dattn, a2, du, gsum, gain2, rows = text_pass(
            x, 0, g1, g2, dmw, dh, (tqkv, text_out, text_up, oqkv, oout, oup), (own, length))
        sums = (
            weight_grad(a2, 0, width, du, hidden, hidden, 512, "up_other", init[0]),
            weight_grad(a1, 0, width, dqkv, 3 * half, 3 * half, 384, "qkv_other", init[1]),
            weight_grad(o, half, half, dattn, 0, width, 256, "out_other", init[2]),
            weight_grad(a2, 0, width, du, 0, hidden, 512, "up_own", init[3]),
            weight_grad(a1, 0, width, dqkv, 0, 3 * half, 384, "qkv_own", init[4]),
            weight_grad(o, 0, half, dattn, 0, width, 256, "out_own", init[5]),
        )
        return sums, gsum, gain2, rows

    groups = dm.shape[0] // 2 // group_pairs
    if groups == 1:
        sums, gsum, gain2, rows = group(rows_x, dmw, dh, (None,) * 6)
    else:
        def one(carry, items):
            sums, gain2, rows = carry
            g, x, dmw, dh = items
            sums, gsum, gain2_new, rows_new = group(x, dmw, dh, sums)
            return (sums, gain2 + gain2_new, jnp.where(g == 0, rows_new, rows)), gsum

        zeros = tuple(
            jnp.zeros(shape, F32)
            for shape in ((width, hidden), (width, 3 * half), (half, width)) * 2
        )
        split = lambda v: v.reshape(groups, -1, v.shape[-1])
        carry = (zeros, jnp.zeros((1, width), F32), jnp.zeros((own, width), F32))
        (sums, gain2, rows), gsum = lax.scan(
            one, carry, (jnp.arange(groups), split(rows_x), split(dmw), split(dh)))
        gsum = gsum.reshape(-1, gsum.shape[-1])
    up_o, qkv_o, out_o, up_m, qkv_m, out_m = sums
    grad_up = up_m + lax.ppermute(up_o, "mp", swap)
    grad_qkv = qkv_m + lax.ppermute(qkv_o, "mp", swap)
    grad_out = out_m + lax.ppermute(out_o, "mp", swap)
    rows_other, gain2_other, gsum_other = lax.ppermute((rows, gain2, gsum[:, hidden:]), "mp", swap)
    grad_rows = jnp.where(core == 0, jnp.concatenate([rows, rows_other], 0), jnp.concatenate([rows_other, rows], 0))
    gsums = jnp.concatenate([gsum[:, :hidden], gsum_other], 0)
    gh, gl = halves(gsums)
    grad_down = tn(gh, dm) + tn(gl, dm)
    grad_proj = tn(low, grad_half)
    gain1 = lax.psum(jnp.sum(grad_qkv * jnp.concatenate([tqkv[0], tqkv[1], tqkv[2]], 1).astype(F32), 1), "mp")
    gain1 = gain1 / text_gain_one
    gain2 = (gain2 + gain2_other)[0]
    part = lambda v: lax.dynamic_slice_in_dim(v, core * half, half, 0)
    return (scal[0, 0], grad_rows.reshape(pair_count, length, width), part(gain1), part(gain2),
            grad_qkv.reshape(width, 3, half), grad_out, grad_up, grad_down, grad_proj, scal[0, 1])


def solution(mesh):
    return jax.shard_map(
        functools.partial(per_device, chip_grid(mesh)),
        mesh=mesh,
        in_specs=(
            P("batch", None, None), P("batch", None, None), P("batch", None), P(None, None, "mp"), P("mp", None),
            P(None, "mp"), P("mp", None), P(), P(), P(None, None, "mp"), P("mp", None), P(None, "mp"), P("mp", None),
            P(None, "mp"), P(),
        ),
        out_specs=(
            P(), P("batch", None, None), P("mp"), P("mp"), P(None, None, "mp"), P("mp", None), P(None, "mp"),
            P("mp", None), P(None, "mp"), P(),
        ),
        check_vma=False,
    )
```

time: 781 us -> 192 us (0.25)
  waiting for transfers between devices: 446 us -> 0.02 us
  blocking collectives: 172 us -> 2.58 us
  Pallas kernels: 0 us -> 152 us
  matrix products: 63.6 us -> 5.16 us
  local copies, waits for them, and re-layouts: 46 us -> 15.3 us
  between operations: 21.4 us -> 1.4 us
  other arithmetic: 30.1 us -> 12 us
    psum x5 -> x0, waiting for transfers between devices: 445 us -> none  [the longest x1 384 us: per_device(): lax.psum((gain_one_part, gain_two_part, grad_qkv, grad_out, grad_up, grad...]
    pallas_call x0 -> x8, Pallas kernels: none -> 152 us  [the longest x1 64.6 us: front(): pl.pallas_call(functools.partial(front_kernel, grid), out_shape=(shape((c...]
    all_gather x3 -> x0, blocking collectives: 82.7 us -> none  [the longest x1 43.2 us: per_device(): image_piece = lax.all_gather(image_norm, 'batch', axis=0, tiled=True)]
    dot_general x29 -> x3, matrix products: 61 us -> 5.16 us  [tn(): lax.dot_general(a, b, (((0,), (0,)), ((), ())), preferred_element_type=F32)]
    psum x2 -> x1, blocking collectives: 49.8 us -> 2.58 us  [per_device(): lax.psum(jnp.sum(grad_qkv * jnp.concatenate([tqkv[0], tqkv[1], tqkv[2]],...]
    unnamed x1 -> x0, blocking collectives: 39.4 us -> none
    reduce_sum x23 -> x1, other arithmetic: 18.8 us -> 2.54 us  [per_device(): jnp.sum(grad_qkv * jnp.concatenate([tqkv[0], tqkv[1], tqkv[2]], 1).astype...]
    unnamed x131 -> x29, local copies, waits for them, and re-layouts: 20.9 us -> 6.45 us
  transfers between devices with their start and end apart: 5 -> 6, of which waited for: 5 -> 0; matrix products, arithmetic and copies ran while one was open for 2% -> 11% of each run, Pallas kernels for 0% -> 14%
where the time goes in v1:
time: 192 us; the launch traced here: 191 us
  Pallas kernels  152 us (79%)
  local copies, waits for them, and re-layouts  15.3 us (8%)
  other arithmetic  12 us (6%)
  matrix products  5.16 us (3%)
  blocking collectives  2.58 us (1%)
  starting transfers between devices  2.32 us (1%)
    pallas_call x1, Pallas kernels, front(): pl.pallas_call(functools.partial(front_kernel, grid), out_shape=(shape((c...  64.6 us
    pallas_call x1, Pallas kernels, text_pass(): pl.pallas_call(text_kernel, grid=(steps,), out_shape=(shape((total, width...  53.2 us
    pallas_call x6, Pallas kernels, weight_grad(): pl.pallas_call(weight_kernel, grid=(g_cols // tile,), out_shape=jax.Shape...  34.6 us
    add x1, other arithmetic, per_device(): grad_up = up_m + lax.ppermute(up_o, 'mp', swap)  6.95 us
    unnamed x29, local copies, waits for them, and re-layouts  6.45 us
    dot_general x3, matrix products, tn(): lax.dot_general(a, b, (((0,), (0,)), ((), ())), preferred_element_type=F32)  5.16 us
  transfers between devices with their start and end apart: 6, of which 0 were waited for; matrix products, arithmetic and copies ran while one was open for 11% of the time, Pallas kernels for 14%

profile of v1, /device:TPU:0, one launch (start us, length us, event | category | flops | bytes accessed | tf_op | source)
XLA Modules:
  0.0 191.1 jit_solution(3698825755583313914)
XLA Ops:
  0.6 1.3 broadcast_in_dim.6.g1_ref
  1.9 1.3 broadcast_in_dim.7.g2_ref
  3.8 64.6 %front.1 = (f32[16,64,768]{2,1,0:T(8,128)}, bf16[3,768,384]{2,1,0:T(8,128)(2,1)}, bf16[384,768]{1,0:T(8,128)(2,1)}, bf16[768,1536]{1,0:T(8,128)(2,1)}, bf16[128,...) custom-call(bf16[128,768]{1,0:T(8,128)(2,1)} %bitcast.31, ...), custom_call_target="tpu_custom_call" | custom-call | tf_op jit(solution)/shard_map/front/pallas_call | solution.py:682
  68.4 53.2 %text_pass.1 = (bf16[1024,768]{1,0:T(8,128)(2,1)}, bf16[1024,2304]{1,0:T(8,128)(2,1)}, bf16[1024,768]{1,0:T(8,128)(2,1)}, bf16[1024,768]{1,0:T(8,128)(2,1)}, bf1...) custom-call(f32[1024,768]{1,0:T(8,128)} %bitcast.27, ...), custom_call_target="tpu_custom_call" | custom-call | tf_op jit(solution)/shard_map/text_pass/pallas_call | solution.py:208
  121.6 6.9 %up_other.1 = f32[768,1536]{1,0:T(8,128)} custom-call(bf16[1024,768]{1,0:T(8,128)(2,1)} %get-tuple-element.42.a_ref, bf16[1024,3072]{1,0:T(8,128)(2,1)} %get-tuple-element.43.g_ref), custom_call_target="tpu_custom_call" | custom-call | tf_op jit(solution)/shard_map/up_other/pallas_call | solution.py:245
  128.5 1.1 collective-permute-start.4
  129.6 0.0 copy-start.9
  129.6 0.0 copy-start.13
  129.6 0.0 copy-start.8
  129.6 0.0 copy-start
  129.6 6.5 %qkv_other.1 = f32[768,1152]{1,0:T(8,128)} custom-call(bf16[1024,768]{1,0:T(8,128)(2,1)} %get-tuple-element.37.a_ref, bf16[1024,2304]{1,0:T(8,128)(2,1)} %get-tuple-element.38.g_ref), custom_call_target="tpu_custom_call" | custom-call | tf_op jit(solution)/shard_map/qkv_other/pallas_call | solution.py:245
  136.0 0.0 collective-permute-start.1
  136.1 0.0 copy-done.9
  136.1 0.5 collective-permute-start
  136.6 0.0 copy-done.13
  136.6 0.1 collective-permute-start.2
  136.6 0.0 copy-done.8
  136.6 0.1 fusion.6
  136.7 0.5 collective-permute-start.5
  137.2 0.0 copy-done
  137.2 1.3 slice_bitcast_fusion.2
  138.5 1.3 fusion.7
  139.8 6.3 %qkv_own.1 = f32[768,1152]{1,0:T(8,128)} custom-call(bf16[1024,768]{1,0:T(8,128)(2,1)} %get-tuple-element.37.a_ref, bf16[1024,2304]{1,0:T(8,128)(2,1)} %get-tuple-element.38.g_ref), custom_call_target="tpu_custom_call" | custom-call | tf_op jit(solution)/shard_map/qkv_own/pallas_call | solution.py:245
  146.1 4.1 %out_own.1 = f32[384,768]{1,0:T(8,128)} custom-call(bf16[1024,768]{1,0:T(8,128)(2,1)} %get-tuple-element.40.a_ref, bf16[1024,768]{1,0:T(8,128)(2,1)} %get-tuple-element.41.g_ref), custom_call_target="tpu_custom_call" | custom-call | tf_op jit(solution)/shard_map/out_own/pallas_call | solution.py:245
  150.1 4.1 %out_other.1 = f32[384,768]{1,0:T(8,128)} custom-call(bf16[1024,768]{1,0:T(8,128)(2,1)} %get-tuple-element.40.a_ref, bf16[1024,768]{1,0:T(8,128)(2,1)} %get-tuple-element.41.g_ref), custom_call_target="tpu_custom_call" | custom-call | tf_op jit(solution)/shard_map/out_other/pallas_call | solution.py:245
  154.2 0.0 copy-start.6
  154.2 0.0 copy-start.10
  154.2 0.0 copy-start.11
  154.2 0.0 copy-start.7
  154.2 6.8 %up_own.1 = f32[768,1536]{1,0:T(8,128)} custom-call(bf16[1024,768]{1,0:T(8,128)(2,1)} %get-tuple-element.42.a_ref, bf16[1024,3072]{1,0:T(8,128)(2,1)} %get-tuple-element.43.g_ref), custom_call_target="tpu_custom_call" | custom-call | tf_op jit(solution)/shard_map/up_own/pallas_call | solution.py:245
  161.1 0.0 collective-permute-done.2
  161.1 0.0 copy-done.6
  161.1 0.1 collective-permute-start.3
  161.2 0.0 copy-done.10
  161.2 0.0 copy-done.11
  161.2 1.4 fusion.8
  162.6 0.6 fusion.3
  163.2 0.0 collective-permute-done
  163.2 0.8 maximum_select_fusion
  163.9 0.0 collective-permute-done.5
  164.0 0.0 copy-done.7
  164.0 0.8 fusion.2
  164.8 0.0 copy-start.2
  164.8 0.0 copy-start.3
  164.8 0.0 copy-start.4
  164.8 0.0 copy-start.5
  164.8 3.0 %convolution_add_fusion = f32[1536,768]{1,0:T(8,128)} fusion(f32[1536,768]{1,0:T(8,128)S(1)} %fusion.2, bf16[128,768]{1,0:T(8,128)(2,1)S(1)} %copy-done.7, f32[64,1536]{1,0:T(8,128)S(1)} %collective-permute-done.5, f32[64,1536]{1,0:T(8,128)S(1)} %get-tuple-element.73), kind=kOutput, calls=%fused_computation | convolution fusion | flops 303955968 | bytes 10420224 | tf_op jit(solution)/shard_map/dot_general | solution.py:27
  167.8 0.0 copy-start.1
  167.8 0.0 collective-permute-done.3
  167.8 0.0 copy-done.2
  167.8 1.1 add.24
  169.0 0.0 collective-permute-done.1
  169.0 0.0 copy-done.3
  169.0 0.0 copy-done.4
  169.0 0.0 copy-done.5
  169.0 1.2 copy-done.1
  170.2 2.5 %multiply_reduce_fusion = (f32[768]{0:T(1024)S(1)}, f32[768,1152]{1,0:T(8,128)S(1)}) fusion(bf16[768,384]{1,0:T(8,128)(2,1)S(1)} %copy-done.4, bf16[768,384]{1,0:T(8,128)(2,1)S(1)} %copy-done.5, bf16[768,384]{1,0:T(8,128)(2,1)S(1)} %copy-done.3, f32[768,1152]{1,0:T(8,128)S(1)} %copy-done.1, f32[768,1152]{1,0:T(8,128)} %collective-permute-done.1), kind=kLoop, calls=%fused_computation.1 | loop fusion | flops 7961856 | bytes 12389376 | tf_op jit(solution)/shard_map/reduce_sum | solution.py:834
  172.8 2.6 %psum.7 = f32[768]{0:T(1024)S(1)} all-reduce(f32[768]{0:T(1024)S(1)} %get-tuple-element.68), channel_id=1, replica_groups=mesh['batch'=16,'mp'=2] {'mp'}, use_global_device_ids=true, to_apply=%region_1.2 | all-reduce | flops 768 | bytes 6144 | tf_op jit(solution)/shard_map/psum | solution.py:834
  175.4 0.0 copy-done.12
  175.4 0.7 dynamic_slice.8
  176.0 3.0 %copy.26 = f32[768,1152]{0,1:T(8,128)} copy(f32[768,1152]{1,0:T(8,128)S(1)} %get-tuple-element.69) | data formatting | bytes 7077888 | tf_op jit(solution)/shard_map/add | solution.py:826
  179.0 5.2 %copy.27 = f32[768,3,384]{2,0,1:T(8,128)} copy(f32[768,3,384]{0,2,1:T(8,128)} %bitcast.26) | data formatting | bytes 7077888
  184.2 0.0 collective-permute-done.4
  184.2 7.0 %add.25 = f32[768,1536]{1,0:T(8,128)} add(f32[768,1536]{1,0:T(8,128)} %up_own.1, f32[768,1536]{1,0:T(8,128)} %collective-permute-done.4) | non-fusion elementwise | flops 1179648 | bytes 14155776 | tf_op jit(solution)/shard_map/add | solution.py:825
  (2 shorter events, 0.0 us)
Async XLA Ops:
  128.5 55.7 %collective-permute-start.4 = (f32[768,1536]{1,0:T(8,128)}, f32[768,1536]{1,0:T(8,128)}, u32[]{:S(2)}, u32[]{:S(2)}) collective-permute-start(f32[768,1536]{1,0:T(8,128)} %up_other.1), channel_id=1, source_target_pairs={{0,1},{1,0},{2,3},{3,2},{4,5},{5,4},{6,7},{7,6},{8,9},{9,8},{10,11... | collective-permute-start | bytes 14155784 | tf_op jit(solution)/shard_map/ppermute | solution.py:825
  129.6 6.5 %copy-start.9 = (f32[64,768]{1,0:T(8,128)S(1)}, f32[64,768]{1,0:T(8,128)}, u32[]{:S(2)}) copy-start(f32[64,768]{1,0:T(8,128)} %get-tuple-element.36) | copy-start | bytes 589828
  129.6 7.0 %copy-start.13 = (f32[1,768]{1,0:T(1,128)S(1)}, f32[1,768]{1,0:T(1,128)}, u32[]{:S(2)}) copy-start(f32[1,768]{1,0:T(1,128)} %get-tuple-element.39) | copy-start | bytes 9220
  129.6 7.1 %copy-start.8 = (f32[64,3072]{1,0:T(8,128)S(1)}, f32[64,3072]{1,0:T(8,128)}, u32[]{:S(2)}) copy-start(f32[64,3072]{1,0:T(8,128)} %get-tuple-element.44) | copy-start | bytes 2359300
  129.6 7.6 %copy-start = (bf16[768,3,384]{2,0,1:T(8,128)(2,1)S(1)}, bf16[768,3,384]{2,0,1:T(8,128)(2,1)}, u32[]{:S(2)}) copy-start(bf16[768,3,384]{2,0,1:T(8,128)(2,1)} %param.24) | copy-start | bytes 5308420
  136.0 32.9 %collective-permute-start.1 = (f32[768,1152]{1,0:T(8,128)}, f32[768,1152]{1,0:T(8,128)}, u32[]{:S(2)}, u32[]{:S(2)}) collective-permute-start(f32[768,1152]{1,0:T(8,128)} %qkv_other.1), channel_id=1, source_target_pairs={{0,1},{1,0},{2,3},{3,2},{4,5},{5,4},{6,7},{7,6},{8,9},{9,8},{10,11... | collective-permute-start | bytes 10616840 | tf_op jit(solution)/shard_map/ppermute | solution.py:826
  136.1 27.1 %collective-permute-start = (f32[64,768]{1,0:T(8,128)S(1)}, f32[64,768]{1,0:T(8,128)S(1)}, u32[]{:S(2)}, u32[]{:S(2)}) collective-permute-start(f32[64,768]{1,0:T(8,128)S(1)} %copy-done.9), channel_id=1, source_target_pairs={{0,1},{1,0},{2,3},{3,2},{4,5},{5,4},{6,7},{7,6},{8,9},{9,8},{10,11... | collective-permute-start | bytes 589832 | tf_op jit(solution)/shard_map/ppermute | solution.py:828
  136.6 24.5 %collective-permute-start.2 = (f32[1,768]{1,0:T(1,128)S(1)}, f32[1,768]{1,0:T(1,128)S(1)}, u32[]{:S(2)}, u32[]{:S(2)}) collective-permute-start(f32[1,768]{1,0:T(1,128)S(1)} %copy-done.13), channel_id=1, source_target_pairs={{0,1},{1,0},{2,3},{3,2},{4,5},{5,4},{6,7},{7,6},{8,9},{9,8},{10,11... | collective-permute-start | bytes 9224 | tf_op jit(solution)/shard_map/ppermute | solution.py:828
  136.7 27.3 %collective-permute-start.5 = (f32[64,1536]{1,0:T(8,128)S(1)}, f32[64,1536]{1,0:T(8,128)S(1)}, u32[]{:S(2)}, u32[]{:S(2)}) collective-permute-start(f32[64,1536]{1,0:T(8,128)S(1)} %get-tuple-element.74), channel_id=1, source_target_pairs={{0,1},{1,0},{2,3},{3,2},{4,5},{5,4},{6,7},{7,6},{8,9},{9,8},{10,11... | collective-permute-start | bytes 1179656 | tf_op jit(solution)/shard_map/ppermute | solution.py:828
  154.2 6.9 %copy-start.6 = (f32[384,768]{1,0:T(8,128)S(1)}, f32[384,768]{1,0:T(8,128)}, u32[]{:S(2)}) copy-start(f32[384,768]{1,0:T(8,128)} %out_other.1) | copy-start | bytes 3538948
  154.2 7.0 %copy-start.10 = (bf16[128,768]{1,0:T(8,128)(2,1)S(1)}, bf16[128,768]{1,0:T(8,128)(2,1)}, u32[]{:S(2)}) copy-start(bf16[128,768]{1,0:T(8,128)(2,1)} %get-tuple-element.46) | copy-start | bytes 589828
  154.2 7.0 %copy-start.11 = (bf16[128,384]{1,0:T(8,128)(2,1)S(1)}, bf16[128,384]{1,0:T(8,128)(2,1)}, u32[]{:S(2)}) copy-start(bf16[128,384]{1,0:T(8,128)(2,1)} %get-tuple-element.47) | copy-start | bytes 294916
  154.2 9.7 %copy-start.7 = (bf16[128,768]{1,0:T(8,128)(2,1)S(1)}, bf16[128,768]{1,0:T(8,128)(2,1)}, u32[]{:S(2)}) copy-start(bf16[128,768]{1,0:T(8,128)(2,1)} %get-tuple-element.45) | copy-start | bytes 589828
  161.1 6.7 %collective-permute-start.3 = (f32[384,768]{1,0:T(8,128)S(1)}, f32[384,768]{1,0:T(8,128)S(1)}, u32[]{:S(2)}, u32[]{:S(2)}) collective-permute-start(f32[384,768]{1,0:T(8,128)S(1)} %copy-done.6), channel_id=1, source_target_pairs={{0,1},{1,0},{2,3},{3,2},{4,5},{5,4},{6,7},{7,6},{8,9},{9,8},{10,11... | collective-permute-start | bytes 3538952 | tf_op jit(solution)/shard_map/ppermute | solution.py:827
  164.8 3.0 %copy-start.2 = (f32[384,768]{1,0:T(8,128)S(1)}, f32[384,768]{1,0:T(8,128)}, u32[]{:S(2)}) copy-start(f32[384,768]{1,0:T(8,128)} %out_own.1) | copy-start | bytes 3538948
  164.8 4.2 %copy-start.3 = (bf16[768,384]{1,0:T(8,128)(2,1)S(1)}, bf16[768,384]{1,0:T(8,128)(2,1)}, u32[]{:S(2)}) copy-start(bf16[768,384]{1,0:T(8,128)(2,1)} %get-tuple-element.70) | copy-start | bytes 1769476
  164.8 4.2 %copy-start.4 = (bf16[768,384]{1,0:T(8,128)(2,1)S(1)}, bf16[768,384]{1,0:T(8,128)(2,1)}, u32[]{:S(2)}) copy-start(bf16[768,384]{1,0:T(8,128)(2,1)} %get-tuple-element.71) | copy-start | bytes 1769476
  164.8 4.2 %copy-start.5 = (bf16[768,384]{1,0:T(8,128)(2,1)S(1)}, bf16[768,384]{1,0:T(8,128)(2,1)}, u32[]{:S(2)}) copy-start(bf16[768,384]{1,0:T(8,128)(2,1)} %get-tuple-element.72) | copy-start | bytes 1769476
  167.8 2.4 %copy-start.1 = (f32[768,1152]{1,0:T(8,128)S(1)}, f32[768,1152]{1,0:T(8,128)}, u32[]{:S(2)}) copy-start(f32[768,1152]{1,0:T(8,128)} %qkv_own.1) | copy-start | bytes 10616836
  170.2 5.1 %copy-start.12 = (f32[768]{0:T(1024)S(1)}, f32[768]{0:T(1024)}, u32[]{:S(2)}) copy-start(f32[768]{0:T(1024)} %param.22) | copy-start | bytes 9220
